TPU v7x, 256 devices: a whole 4x4x8 slice. The times are simulated.
256 devices in a mesh: gx: 32 (over x, y, z_hi), gy: 8 (over z_lo, core).
Axes of the slice: x: 4, y: 4, z: 8 (z_hi: 2, z_lo: 4; z = z_hi * 4 + z_lo), core: 2. Of those that a mesh axis runs over, the one named last changes fastest.
Arguments:
- scalars: bfloat16 [32, 8, 256, 2048], P('gx', 'gy'), may hold values from -6 to 6
- tensors: bfloat16 [32, 8, 9, 64, 2048], P('gx', 'gy'), may hold values from -6 to 6
- vectors: float32 [32, 8, 3, 2048], P('gx', 'gy'), may hold values from -1 to 1
- species: int32 [32, 8, 2048], P('gx', 'gy'), may hold values from 0 to 3
- species_table: float32 [256, 4], replicated, may hold values from -3 to 3
- reverse: int32 [32, 8, 2048], P('gx', 'gy'), may hold values from 0 to 2559, as said below
- send_index: int32 [32, 8, 8, 64], P('gx', 'gy'), may hold values from 0 to 2047, as said below
- counts: int32 [32, 8, 8], P('gx', 'gy'), may hold values from 32 to 64, as said below
- w_query: bfloat16 [256, 256], replicated, may hold values from -0.375 to 0.375
- w_key: bfloat16 [256, 256], replicated, may hold values from -0.375 to 0.375
- w_value: bfloat16 [256, 256], replicated, may hold values from -0.375 to 0.375
- w_output: bfloat16 [256, 256], replicated, may hold values from -0.375 to 0.375
- w_invariant: bfloat16 [256, 192], replicated, may hold values from -0.4375 to 0.4375
- w_message: bfloat16 [256, 256], replicated, may hold values from -0.375 to 0.375
- w_gate: bfloat16 [192, 256], replicated, may hold values from -0.375 to 0.375
- w_radial: bfloat16 [192, 256], replicated, may hold values from -0.375 to 0.375
- w_mixing: bfloat16 [64, 64], replicated, may hold values from -0.75 to 0.75
- w_expand: bfloat16 [512, 256], replicated, may hold values from -0.375 to 0.375
- w_reverse: bfloat16 [512, 256], replicated, may hold values from -0.375 to 0.375
- w_contract: bfloat16 [256, 512], replicated, may hold values from -0.25 to 0.25
Outputs:
- new_scalars: bfloat16 [32, 8, 256, 2048], P('gx', 'gy')
- new_tensors: bfloat16 [32, 8, 9, 64, 2048], P('gx', 'gy')
Inputs may be any that keep to these rules, and one draw needn't show every extreme that they name: counts[p] of a domain equals the count of its partner in direction p toward it (the opposite direction); some domain has 64 live slots toward some partner in every direction. `send_index`: live slots of a domain name distinct edges; slots at or above the count hold 0. The edge in live slot s of block p has as reverse slot s of the block received in the opposite direction; every live received slot is named by exactly one edge, no empty slot is named, and the other edges are paired among themselves (at most one edge of a domain is its own reverse).
All inputs are finite; a program needn't handle non-finite values.
Results may differ from a plain program's by a relative error of at most 0.01.
Values may be sent and summed in bfloat16 or wider, within the bound.
A program may use at most 64 MiB of HBM per device.

v0:
```python
import functools
import math

import jax
import jax.numpy as jnp
from jax import lax
from jax.experimental import pallas as pl
from jax.experimental.pallas import tpu as pltpu
from jax.sharding import PartitionSpec as P

MESH = pl.DeviceIdType.MESH
HEADS = 8
DIRECTIONS = ((1, 0), (-1, 0), (0, 1), (0, -1), (1, 1), (1, -1), (-1, 1), (-1, -1))
OPPOSITE = (1, 0, 3, 2, 7, 6, 5, 4)
C = 256
MUL = 64
ROWS_T = 9 * MUL
ROWS = C + ROWS_T
FFN = 512
E = 2048
BLOCK = 64
SLOTS = 8 * BLOCK
EXTRA = 16
TILE = 256
PAIR = 2 * BLOCK
GROUPS = SLOTS // PAIR
DEGREE = (0, 1, 1, 1, 2, 2, 2, 2, 2)
BF = jnp.bfloat16
F32 = jnp.float32


def dot(a, b):
    return jnp.dot(a, b, preferred_element_type=F32)


def sigmoid(v):
    return 0.5 * jnp.tanh(0.5 * v) + 0.5


def one_hot(rows, first, ids):
    iota = lax.broadcasted_iota(jnp.int32, (rows, ids.shape[1]), 0)
    return jnp.where(iota == ids - first, 1.0, 0.0).astype(BF)


def slot_of(reverse):
    away = reverse - E
    block = lax.shift_right_logical(away, 6)
    partner = jnp.where(block < 4, jnp.bitwise_xor(block, 1), 11 - block)
    return jnp.where(reverse < E, -1, partner * BLOCK + jnp.bitwise_and(away, BLOCK - 1))


def harmonics(x, y, z):
    r2 = x * x + y * y + z * z
    root = math.sqrt(3.0)
    return (None, x, y, z, root * x * y, root * y * z, 0.5 * (3.0 * z * z - r2), root * x * z, 0.5 * root * (x * x - y * y))


def embed(scalars, table, species):
    n = scalars.shape[1]
    parts = []
    for lane in range(0, n, 128):
        sp = species[:, lane : lane + 128]
        t = [table[j] for j in range(4)]
        low = jnp.where(sp == 0, t[0], t[1])
        high = jnp.where(sp == 2, t[2], t[3])
        parts.append(scalars[:, lane : lane + 128].astype(F32) + jnp.where(sp < 2, low, high))
    return (parts[0] if len(parts) == 1 else jnp.concatenate(parts, axis=1)).astype(BF)


def invariants(tensors, tensors_rev):
    sums = [None, None, None]
    for k in range(9):
        term = tensors(k).astype(F32) * tensors_rev(k).astype(F32)
        d = DEGREE[k]
        sums[d] = term if sums[d] is None else sums[d] + term
    return jnp.concatenate(sums, axis=0).astype(BF)


def middle_of(embedded, scalars_rev, invariant, wq, wkv, wo, wi):
    n = embedded.shape[1]
    head = C // HEADS
    queries = dot(wq[...], embedded)
    kv = dot(wkv[...], scalars_rev)
    scores = jnp.sum((queries * kv[:C]).reshape(HEADS, head, n), axis=1, keepdims=True)
    attention = sigmoid(scores * (1.0 / math.sqrt(head)))
    attended = (attention * kv[C:].reshape(HEADS, head, n)).reshape(C, n).astype(BF)
    return (embedded.astype(F32) + dot(wo[...], attended) + dot(wi[...], invariant)).astype(BF)


def update_tensors(k, tensor, tensor_rev, gate, radial, harmonic, wx):
    d = DEGREE[k]
    rows = slice(d * MUL, (d + 1) * MUL)
    mixed = dot(wx[...], tensor_rev)
    last = radial[rows] if harmonic is None else radial[rows] * harmonic
    return (tensor.astype(F32) + gate[rows] * mixed + last).astype(BF)


def feed_forward(middle, incoming, wer, wc):
    v = dot(wer[...], jnp.concatenate([middle, incoming], axis=0))
    hidden = (v * sigmoid(v)).astype(BF)
    return (middle.astype(F32) + dot(wc[...], hidden)).astype(BF)


def exchange_kernel(
    nx, ny,
    scalars_h, tensors_h, vectors_h, species_h, table_h, reverse_h, send_h,
    wq_h, wk_h, wv_h, wo_h, wi_h, wm_h, wg_h, wr_h, wx_h, we_h, wrev_h, wc_h,
    part_h, last_h,
    x, xe, vec, spc, tab, rev, sidx,
    wq, wkv, wo, wit, wi, wmgr, wx, wer, wc,
    g, p, rev_t, own, send_a, send_b, recv_a, recv_b, send_s, recv_s,
    mid, msg, out, y, tb,
    load_sem, send_sem, recv_sem, store_sem,
):
    gx, gy = lax.axis_index("gx"), lax.axis_index("gy")
    partners = [(lax.rem(gx + dx + nx, nx), lax.rem(gy + dy + ny, ny)) for dx, dy in DIRECTIONS]
    barrier = pltpu.get_barrier_semaphore()
    for partner in partners:
        pl.semaphore_signal(barrier, inc=1, device_id=partner, device_id_type=MESH)

    loads = {}

    def load(name, src, dst):
        copy = pltpu.make_async_copy(src, dst, load_sem.at[len(loads)])
        copy.start()
        loads[name] = copy

    load("send", send_h, sidx)
    load("scalars", scalars_h, x.at[pl.ds(0, C)])
    load("tensors", tensors_h, x.at[pl.ds(C, ROWS_T)])
    load("vectors", vectors_h, vec)
    load("species", species_h, spc)
    load("reverse", reverse_h, rev)
    load("table", table_h, tab)
    load("wq", wq_h, wq)
    load("wk", wk_h, wkv.at[pl.ds(0, C)])
    load("wv", wv_h, wkv.at[pl.ds(C, C)])
    load("wo", wo_h, wo)
    load("wi", wi_h, wit)
    load("wm", wm_h, wmgr.at[pl.ds(0, C)])
    load("wg", wg_h, wmgr.at[pl.ds(C, 3 * MUL)])
    load("wr", wr_h, wmgr.at[pl.ds(C + 3 * MUL, 3 * MUL)])
    load("wx", wx_h, wx)
    load("we", we_h, wer.at[:, pl.ds(0, C)])
    load("wrev", wrev_h, wer.at[:, pl.ds(C, C)])
    load("wc", wc_h, wc)

    loads["send"].wait()
    lane = lax.broadcasted_iota(jnp.int32, (1, PAIR), 1)

    def ids_of(pair):
        a, b = sidx[2 * pair : 2 * pair + 1, :], sidx[2 * pair + 1 : 2 * pair + 2, :]
        return jnp.concatenate([a, b], axis=1)

    def pack(block, pair, dst):
        h = block.shape[0] // 2
        top, bottom = block[:h], block[h:]
        dst[2 * pair] = jnp.where(lane < BLOCK, top, pltpu.roll(bottom, BLOCK, 1)).astype(BF)
        dst[2 * pair + 1] = jnp.where(lane < BLOCK, pltpu.roll(top, BLOCK, 1), bottom).astype(BF)

    copies_a, copies_b, copies_s = [], [], []
    for d in range(8):
        o = OPPOSITE[d]
        for kind, (copies, src, dst) in enumerate(
            (
                (copies_a, send_a.at[d], recv_a.at[o]),
                (copies_b, send_b.at[d], recv_b.at[o]),
                (copies_s, send_s.at[pl.ds(d, 1)], recv_s.at[pl.ds(o, 1)]),
            )
        ):
            copies.append(
                pltpu.make_async_remote_copy(
                    src_ref=src,
                    dst_ref=dst,
                    send_sem=send_sem.at[kind, d],
                    recv_sem=recv_sem.at[kind, o],
                    device_id=partners[d],
                    device_id_type=MESH,
                )
            )

    for half in range(2):
        cols = pl.ds(half * TILE, TILE)
        ids = jnp.concatenate([ids_of(2 * half), ids_of(2 * half + 1)], axis=1)
        g[:, cols] = one_hot(E, 0, ids)
        if half == 0:
            loads["scalars"].wait()
        picked = dot(x[pl.ds(0, C)], g[:, cols])
        own[pl.ds(0, C), cols] = picked.astype(BF)
        for j in range(2):
            pack(picked[:, j * PAIR : (j + 1) * PAIR], 2 * half + j, send_a)
        if half == 0:
            pl.semaphore_wait(barrier, 8)
        for d in range(4 * half, 4 * half + 4):
            copies_a[d].start()
        if half == 0:
            loads["tensors"].wait()
        picked = dot(x[pl.ds(C, ROWS_T)], g[:, cols])
        own[pl.ds(C, ROWS_T), cols] = picked.astype(BF)
        for j in range(2):
            pack(picked[:, j * PAIR : (j + 1) * PAIR], 2 * half + j, send_b)
        for d in range(4 * half, 4 * half + 4):
            copies_b[d].start()

    loads["vectors"].wait()
    loads["species"].wait()
    v = [vec[k] for k in range(3)]
    high = [u.astype(BF).astype(F32) for u in v]
    middle = [(a - b).astype(BF).astype(F32) for a, b in zip(v, high)]
    low = [a - b - c for a, b, c in zip(v, high, middle)]
    species_row = spc[...].astype(F32)
    xe[...] = jnp.concatenate(high + middle + low + [species_row] + [jnp.zeros_like(species_row)] * (EXTRA - 10), axis=0).astype(BF)
    extra = dot(xe[...], g[...])
    own_vec = [extra[k : k + 1] + (extra[3 + k : 4 + k] + extra[6 + k : 7 + k]) for k in range(3)]
    own_species = extra[9:10]
    for pair in range(GROUPS):
        s = own_species[:, pair * PAIR : (pair + 1) * PAIR]
        send_s[2 * pair : 2 * pair + 1] = s
        send_s[2 * pair + 1 : 2 * pair + 2] = pltpu.roll(s, BLOCK, 1)
    for d in range(8):
        copies_s[d].start()

    loads["table"].wait()
    for j in range(4):
        for h in range(2):
            row = tab[j : j + 1, h * 128 : (h + 1) * 128]
            tb[j, pl.ds(h * 128, 128)] = jnp.broadcast_to(row, (128, 128)).T
    for name in ("reverse", "wq", "wk", "wv", "wo", "wi", "wm", "wg", "wr", "wx", "we", "wrev", "wc"):
        loads[name].wait()
    wi[...] = wit[...].astype(F32).T.astype(BF)

    def first_tile(t, carry):
        cols = pl.ds(pl.multiple_of(t * TILE, TILE), TILE)
        ids = rev[:, cols]
        p[:, cols] = one_hot(E, 0, ids)
        rev_t[...] = dot(x[...], p[:, cols]).astype(BF)
        embedded = embed(x[pl.ds(0, C), cols], tb, spc[:, cols])
        invariant = invariants(
            lambda k: x[pl.ds(C + k * MUL, MUL), cols], lambda k: rev_t[pl.ds(C + k * MUL, MUL)]
        )
        m = middle_of(embedded, rev_t[pl.ds(0, C)], invariant, wq, wkv, wo, wi)
        mid[:, cols] = m
        mgr = dot(wmgr[...], m)
        msg[:, cols] = mgr[:C].astype(BF)
        gate = sigmoid(mgr[C : C + 3 * MUL])
        radial = mgr[C + 3 * MUL :]
        harmonic = harmonics(vec[0, :, cols], vec[1, :, cols], vec[2, :, cols])
        local = ids < E
        for k in range(9):
            rows = pl.ds(C + k * MUL, MUL)
            new = update_tensors(k, x[rows, cols], rev_t[rows], gate, radial, harmonic[k], wx)
            out[rows, cols] = jnp.where(local, new.astype(F32), 0.0).astype(BF)
        return carry

    lax.fori_loop(0, E // TILE, first_tile, 0)

    def second_tile(t, carry):
        cols = pl.ds(pl.multiple_of(t * TILE, TILE), TILE)
        incoming = dot(msg[...], p[:, cols]).astype(BF)
        new = feed_forward(mid[:, cols], incoming, wer, wc)
        out[pl.ds(0, C), cols] = jnp.where(rev[:, cols] < E, new.astype(F32), 0.0).astype(BF)
        return carry

    lax.fori_loop(0, E // TILE, second_tile, 0)

    def unpack(a, b):
        a, b = a.astype(F32), b.astype(F32)
        top = jnp.where(lane < BLOCK, a, pltpu.roll(b, BLOCK, 1))
        bottom = jnp.where(lane < BLOCK, pltpu.roll(a, BLOCK, 1), b)
        return jnp.concatenate([top, bottom], axis=0).astype(BF)

    for pair in range(GROUPS):
        cols = pl.ds(pair * PAIR, PAIR)
        for d in (2 * pair, 2 * pair + 1):
            copies_a[OPPOSITE[d]].wait_recv()
            copies_s[OPPOSITE[d]].wait_recv()
        here = own[pl.ds(0, C), cols]
        there = unpack(recv_a[2 * pair], recv_a[2 * pair + 1])
        species_there = jnp.where(
            lane < BLOCK, recv_s[2 * pair : 2 * pair + 1], pltpu.roll(recv_s[2 * pair + 1 : 2 * pair + 2], BLOCK, 1)
        )
        species_both = jnp.concatenate([own_species[:, pair * PAIR : (pair + 1) * PAIR], species_there], axis=1)
        embedded = embed(jnp.concatenate([here, there], axis=1), tb, species_both)
        for d in (2 * pair, 2 * pair + 1):
            copies_b[OPPOSITE[d]].wait_recv()
        rev_t[pl.ds(C, ROWS_T), pl.ds(0, PAIR)] = unpack(recv_b[2 * pair], recv_b[2 * pair + 1])
        invariant = invariants(
            lambda k: own[pl.ds(C + k * MUL, MUL), cols], lambda k: rev_t[pl.ds(C + k * MUL, MUL), pl.ds(0, PAIR)]
        )
        m = middle_of(
            embedded,
            jnp.concatenate([there, here], axis=1),
            jnp.concatenate([invariant, invariant], axis=1),
            wq, wkv, wo, wi,
        )
        mgr = dot(wmgr[...], m)
        gate = sigmoid(mgr[C : C + 3 * MUL, :PAIR])
        radial = mgr[C + 3 * MUL :, :PAIR]
        harmonic = harmonics(*[u[:, pair * PAIR : (pair + 1) * PAIR] for u in own_vec])
        for k in range(9):
            rows = pl.ds(C + k * MUL, MUL)
            y[rows, cols] = update_tensors(
                k, own[rows, cols], rev_t[rows, pl.ds(0, PAIR)], gate, radial, harmonic[k], wx
            )
        y[pl.ds(0, C), cols] = feed_forward(m[:, :PAIR], mgr[:C, PAIR:].astype(BF), wer, wc)
        if pair == GROUPS - 2:
            done = (pair + 1) * PAIR

            def place(t, carry):
                tile = pl.ds(pl.multiple_of(t * TILE, TILE), TILE)
                hot = one_hot(done, 0, slot_of(rev[:, tile]))
                add = dot(y[:, pl.ds(0, done)], hot)
                out[:, tile] = (out[:, tile].astype(F32) + add).astype(BF)
                return carry

            lax.fori_loop(0, E // TILE, place, 0)
            store = pltpu.make_async_copy(out, part_h, store_sem.at[0])
            store.start()
    last = pltpu.make_async_copy(y.at[:, pl.ds((GROUPS - 1) * PAIR, PAIR)], last_h, store_sem.at[1])
    last.start()
    for d in range(8):
        copies_a[d].wait_send()
        copies_b[d].wait_send()
        copies_s[d].wait_send()
    store.wait()
    last.wait()


CHUNKS = (64, 192, 192, 192, 192)


def final_kernel(part_h, last_h, reverse_h, scalars_h, tensors_h, part, last, rev, hot, load_sem, store_sem):
    loads = []

    def load(src, dst):
        copy = pltpu.make_async_copy(src, dst, load_sem.at[len(loads)])
        copy.start()
        loads.append(copy)

    load(reverse_h, rev)
    load(last_h, last)
    starts = [sum(CHUNKS[:i]) for i in range(len(CHUNKS))]
    for start, rows in zip(starts, CHUNKS):
        load(part_h.at[pl.ds(start, rows)], part.at[pl.ds(start, rows)])
    loads[0].wait()
    hot[...] = one_hot(PAIR, (GROUPS - 1) * PAIR, slot_of(rev[...]))
    loads[1].wait()
    stores = []
    for i, (start, rows) in enumerate(zip(starts, CHUNKS)):
        loads[2 + i].wait()
        for t in range(0, E, 512):
            add = dot(last[pl.ds(start, rows)], hot[:, pl.ds(t, 512)])
            part[pl.ds(start, rows), pl.ds(t, 512)] = (part[pl.ds(start, rows), pl.ds(t, 512)].astype(F32) + add).astype(BF)
        dst = scalars_h.at[pl.ds(start, rows)] if start < C else tensors_h.at[pl.ds(start - C, rows)]
        copy = pltpu.make_async_copy(part.at[pl.ds(start, rows)], dst, store_sem.at[i])
        copy.start()
        stores.append(copy)
    for copy in stores:
        copy.wait()


def per_device(
    nx, ny,
    scalars, tensors, vectors, species, species_table, reverse, send_index, counts,
    w_query, w_key, w_value, w_output, w_invariant, w_message, w_gate, w_radial, w_mixing, w_expand, w_reverse, w_contract,
):
    reverse_row = reverse.reshape(1, E)
    hbm = pl.BlockSpec(memory_space=pltpu.HBM)
    part, last = pl.pallas_call(
        functools.partial(exchange_kernel, nx, ny),
        out_shape=(jax.ShapeDtypeStruct((ROWS, E), BF), jax.ShapeDtypeStruct((ROWS, PAIR), BF)),
        in_specs=[hbm] * 19,
        out_specs=(hbm, hbm),
        scratch_shapes=[
            pltpu.VMEM((ROWS, E), BF),
            pltpu.VMEM((EXTRA, E), BF),
            pltpu.VMEM((3, 1, E), F32),
            pltpu.VMEM((1, E), jnp.int32),
            pltpu.VMEM((4, C), F32),
            pltpu.VMEM((1, E), jnp.int32),
            pltpu.VMEM((8, BLOCK), jnp.int32),
            pltpu.VMEM((C, C), BF),
            pltpu.VMEM((2 * C, C), BF),
            pltpu.VMEM((C, C), BF),
            pltpu.VMEM((3 * MUL, C), BF),
            pltpu.VMEM((C, 3 * MUL), BF),
            pltpu.VMEM((C + 6 * MUL, C), BF),
            pltpu.VMEM((MUL, MUL), BF),
            pltpu.VMEM((FFN, 2 * C), BF),
            pltpu.VMEM((C, FFN), BF),
            pltpu.VMEM((E, SLOTS), BF),
            pltpu.VMEM((E, E), BF),
            pltpu.VMEM((ROWS, TILE), BF),
            pltpu.VMEM((ROWS, SLOTS), BF),
            pltpu.VMEM((8, C // 2, 128), BF),
            pltpu.VMEM((8, ROWS_T // 2, 128), BF),
            pltpu.VMEM((8, C // 2, 128), BF),
            pltpu.VMEM((8, ROWS_T // 2, 128), BF),
            pltpu.VMEM((8, 128), F32),
            pltpu.VMEM((8, 128), F32),
            pltpu.VMEM((C, E), BF),
            pltpu.VMEM((C, E), BF),
            pltpu.VMEM((ROWS, E), BF),
            pltpu.VMEM((ROWS, SLOTS), BF),
            pltpu.VMEM((4, C, 128), F32),
            pltpu.SemaphoreType.DMA((19,)),
            pltpu.SemaphoreType.DMA((3, 8)),
            pltpu.SemaphoreType.DMA((3, 8)),
            pltpu.SemaphoreType.DMA((2,)),
        ],
        compiler_params=pltpu.CompilerParams(collective_id=0, has_side_effects=True, vmem_limit_bytes=int(60 * 2**20)),
        cost_estimate=pl.CostEstimate(flops=16 * 10**9, bytes_accessed=9 * 2**20, transcendentals=3 * 10**6),
        name="exchange",
    )(
        scalars.reshape(C, E), tensors.reshape(ROWS_T, E), vectors.reshape(3, 1, E), species.reshape(1, E),
        species_table.T, reverse_row, send_index.reshape(8, BLOCK),
        w_query, w_key, w_value, w_output, w_invariant.T, w_message, w_gate, w_radial, w_mixing,
        w_expand, w_reverse, w_contract,
    )
    new_scalars, new_tensors = pl.pallas_call(
        final_kernel,
        out_shape=(jax.ShapeDtypeStruct((C, E), BF), jax.ShapeDtypeStruct((ROWS_T, E), BF)),
        in_specs=[hbm] * 3,
        out_specs=(hbm, hbm),
        scratch_shapes=[
            pltpu.VMEM((ROWS, E), BF),
            pltpu.VMEM((ROWS, PAIR), BF),
            pltpu.VMEM((1, E), jnp.int32),
            pltpu.VMEM((PAIR, E), BF),
            pltpu.SemaphoreType.DMA((2 + len(CHUNKS),)),
            pltpu.SemaphoreType.DMA((len(CHUNKS),)),
        ],
        compiler_params=pltpu.CompilerParams(vmem_limit_bytes=int(56 * 2**20)),
        cost_estimate=pl.CostEstimate(flops=10**9, bytes_accessed=7 * 2**20, transcendentals=0),
        name="combine",
    )(part, last, reverse_row)
    return new_scalars.reshape(1, 1, C, E), new_tensors.reshape(1, 1, 9, MUL, E)


def solution(mesh):
    split = P("gx", "gy")
    return jax.shard_map(
        functools.partial(per_device, mesh.shape["gx"], mesh.shape["gy"]),
        mesh=mesh,
        in_specs=(split,) * 4 + (P(),) + (split,) * 3 + (P(),) * 12,
        out_specs=(split, split),
        check_vma=False,
    )
```

profile of v0, /device:TPU:1, one launch (start us, length us, event | category | flops | bytes accessed | tf_op | source)
XLA Modules:
  0.0 58.6 jit_solution(13298228107347185491)
XLA Ops:
  0.6 54.1 %exchange.1 = (bf16[832,2048]{1,0:T(8,128)(2,1)}, bf16[832,128]{1,0:T(8,128)(2,1)}) custom-call(bf16[256,2048]{1,0:T(8,128)(2,1)} %bitcast.11, bf16[576,2048]{1,0:T(8,128)(2,1)} %bitcast.10, f32[3,1,2048]{2,1,0:T(1,128)} %bitcast.13, s32[1,2048]{1,0:T(1,128)} %bitcast.14, f32[4,256]{1,0:T(4,128)} %bitcast.17, s32[1,2048]{1,0:T(1,128)} %bitcast.15, ...), custom_call_target="tpu_custom_call" | custom-call | flops 16000000000 | bytes 9437184 | tf_op jit(solution)/shard_map/exchange/pallas_call | solution.py:369
  54.7 3.7 %combine.1 = (bf16[256,2048]{1,0:T(8,128)(2,1)}, bf16[576,2048]{1,0:T(8,128)(2,1)}) custom-call(bf16[832,2048]{1,0:T(8,128)(2,1)} %get-tuple-element.6.part_h, bf16[832,128]{1,0:T(8,128)(2,1)} %get-tuple-element.7.last_h, s32[1,2048]{1,0:T(1,128)} %bitcast.16), custom_call_target="tpu_custom_call" | custom-call | flops 1000000000 | bytes 7340032 | tf_op jit(solution)/shard_map/combine/pallas_call | solution.py:420
where the time goes:
time: 58.8 us; the launch traced here: 58.6 us
  Pallas kernels  57.8 us (98%)
  between operations  0.81 us (1%)
    pallas_call x1, Pallas kernels, per_device(): pl.pallas_call(functools.partial(exchange_kernel, nx, ny), out_shape=(jax...  54.1 us
    pallas_call x1, Pallas kernels, per_device(): pl.pallas_call(final_kernel, out_shape=(jax.ShapeDtypeStruct((C, E), BF),...  3.74 us

commit v1 on v0

v1 whole, which is shorter than its diff:
```python
import functools
import math

import jax
import jax.numpy as jnp
from jax import lax
from jax.experimental import pallas as pl
from jax.experimental.pallas import tpu as pltpu
from jax.sharding import PartitionSpec as P

MESH = pl.DeviceIdType.MESH
HEADS = 8
DIRECTIONS = ((1, 0), (-1, 0), (0, 1), (0, -1), (1, 1), (1, -1), (-1, 1), (-1, -1))
OPPOSITE = (1, 0, 3, 2, 7, 6, 5, 4)
C = 256
MUL = 64
ROWS_T = 9 * MUL
ROWS = C + ROWS_T
FFN = 512
E = 2048
BLOCK = 64
SLOTS = 8 * BLOCK
EXTRA = 16
TILE = 256
PAIR = 2 * BLOCK
GROUPS = SLOTS // PAIR
ARRIVAL = (0, 1, 3, 2)
EARLY = 2 * PAIR
DEGREE = (0, 1, 1, 1, 2, 2, 2, 2, 2)
BF = jnp.bfloat16
F32 = jnp.float32


def dot(a, b):
    return jnp.dot(a, b, preferred_element_type=F32)


def sigmoid(v):
    return 0.5 * jnp.tanh(0.5 * v) + 0.5


def one_hot(rows, first, ids):
    iota = lax.broadcasted_iota(jnp.int32, (rows, ids.shape[1]), 0)
    return jnp.where(iota == ids - first, 1.0, 0.0).astype(BF)


def slot_of(reverse):
    away = reverse - E
    block = lax.shift_right_logical(away, 6)
    partner = jnp.where(block < 4, jnp.bitwise_xor(block, 1), 11 - block)
    return jnp.where(reverse < E, -1, partner * BLOCK + jnp.bitwise_and(away, BLOCK - 1))


def harmonics(x, y, z):
    r2 = x * x + y * y + z * z
    root = math.sqrt(3.0)
    return (None, x, y, z, root * x * y, root * y * z, 0.5 * (3.0 * z * z - r2), root * x * z, 0.5 * root * (x * x - y * y))


def embed(scalars, table, species):
    n = scalars.shape[1]
    parts = []
    for lane in range(0, n, 128):
        sp = species[:, lane : lane + 128]
        t = [table[j] for j in range(4)]
        low = jnp.where(sp == 0, t[0], t[1])
        high = jnp.where(sp == 2, t[2], t[3])
        parts.append(scalars[:, lane : lane + 128].astype(F32) + jnp.where(sp < 2, low, high))
    return (parts[0] if len(parts) == 1 else jnp.concatenate(parts, axis=1)).astype(BF)


def invariants(tensors, tensors_rev):
    sums = [None, None, None]
    for k in range(9):
        term = tensors(k).astype(F32) * tensors_rev(k).astype(F32)
        d = DEGREE[k]
        sums[d] = term if sums[d] is None else sums[d] + term
    return jnp.concatenate(sums, axis=0).astype(BF)


def edge_update(tensors, tensors_rev, embedded, scalars_turned, harmonic, wq, wkv, wo, wi, wm, wgr, wx, wer, wc, store):
    n = embedded.shape[1] // 2
    head = C // HEADS
    queries = dot(wq[...], embedded)
    kv = dot(wkv[...], scalars_turned)
    scores = jnp.sum((queries * kv[:C]).reshape(HEADS, head, 2 * n), axis=1, keepdims=True)
    attention = sigmoid(scores * (1.0 / math.sqrt(head)))
    attended = (attention * kv[C:].reshape(HEADS, head, 2 * n)).reshape(C, 2 * n).astype(BF)
    shared = dot(wi[...], invariants(tensors, tensors_rev))
    middles = (embedded.astype(F32) + dot(wo[...], attended) + jnp.concatenate([shared, shared], axis=1)).astype(BF)
    middle = middles[:, :n]
    incoming = dot(wm[...], middles[:, n:]).astype(BF)
    gr = dot(wgr[...], middle)
    for k in range(9):
        d = DEGREE[k]
        mixed = dot(wx[...], tensors_rev(k))
        gate = sigmoid(gr[d * MUL : (d + 1) * MUL])
        radial = gr[(3 + d) * MUL : (4 + d) * MUL]
        last = radial if harmonic[k] is None else radial * harmonic[k]
        store(k, (tensors(k).astype(F32) + gate * mixed + last).astype(BF))
    v = dot(wer[...], jnp.concatenate([middle, incoming], axis=0))
    hidden = (v * sigmoid(v)).astype(BF)
    store(-1, (middle.astype(F32) + dot(wc[...], hidden)).astype(BF))


def exchange_kernel(
    nx, ny,
    scalars_h, tensors_h, vectors_h, species_h, table_h, reverse_h, send_h,
    wq_h, wk_h, wv_h, wo_h, wi_h, wm_h, wg_h, wr_h, wx_h, we_h, wrev_h, wc_h,
    out, y_late,
    x, vec, spc, tab, rev, sidx,
    wq, wkv, wo, wit, wi, wm, wgr, wx, wer, wc,
    g, p0, p1, rev0, rev1, own, send_a, send_b, recv_a, recv_b, send_s, recv_s,
    y, tb,
    load_sem, send_sem, recv_sem,
):
    gx, gy = lax.axis_index("gx"), lax.axis_index("gy")
    partners = [(lax.rem(gx + dx + nx, nx), lax.rem(gy + dy + ny, ny)) for dx, dy in DIRECTIONS]
    barrier = pltpu.get_barrier_semaphore()
    for partner in partners:
        pl.semaphore_signal(barrier, inc=1, device_id=partner, device_id_type=MESH)

    loads = {}

    def load(name, src, dst):
        copy = pltpu.make_async_copy(src, dst, load_sem.at[len(loads)])
        copy.start()
        loads[name] = copy

    load("send", send_h, sidx)
    load("scalars", scalars_h, x.at[pl.ds(0, C)])
    load("tensors", tensors_h, x.at[pl.ds(C, ROWS_T)])
    load("vectors", vectors_h, vec)
    load("species", species_h, spc)

    loads["send"].wait()
    lane = lax.broadcasted_iota(jnp.int32, (1, PAIR), 1)

    def ids_of(pair):
        a, b = sidx[2 * pair : 2 * pair + 1, :], sidx[2 * pair + 1 : 2 * pair + 2, :]
        return jnp.concatenate([a, b], axis=1)

    def pack(block, pair, dst):
        h = block.shape[0] // 2
        top, bottom = block[:h], block[h:]
        dst[2 * pair] = jnp.where(lane < BLOCK, top, pltpu.roll(bottom, BLOCK, 1)).astype(BF)
        dst[2 * pair + 1] = jnp.where(lane < BLOCK, pltpu.roll(top, BLOCK, 1), bottom).astype(BF)

    copies_a, copies_b, copies_s = [], [], []
    for d in range(8):
        o = OPPOSITE[d]
        for kind, (copies, src, dst) in enumerate(
            (
                (copies_a, send_a.at[d], recv_a.at[o]),
                (copies_b, send_b.at[d], recv_b.at[o]),
                (copies_s, send_s.at[pl.ds(d, 1)], recv_s.at[pl.ds(o, 1)]),
            )
        ):
            copies.append(
                pltpu.make_async_remote_copy(
                    src_ref=src,
                    dst_ref=dst,
                    send_sem=send_sem.at[kind, d],
                    recv_sem=recv_sem.at[kind, o],
                    device_id=partners[d],
                    device_id_type=MESH,
                )
            )

    for half in range(2):
        cols = pl.ds(half * TILE, TILE)
        ids = jnp.concatenate([ids_of(2 * half), ids_of(2 * half + 1)], axis=1)
        g[:, cols] = one_hot(E, 0, ids)
        if half == 0:
            loads["scalars"].wait()
        picked = dot(x[pl.ds(0, C)], g[:, cols])
        own[pl.ds(0, C), cols] = picked.astype(BF)
        for j in range(2):
            pack(picked[:, j * PAIR : (j + 1) * PAIR], 2 * half + j, send_a)
        if half == 0:
            pl.semaphore_wait(barrier, 8)
        for d in range(4 * half, 4 * half + 4):
            copies_a[d].start()
        if half == 0:
            load("reverse", reverse_h, rev)
            load("table", table_h, tab)
            load("wq", wq_h, wq)
            load("wk", wk_h, wkv.at[pl.ds(0, C)])
            load("wv", wv_h, wkv.at[pl.ds(C, C)])
            load("wo", wo_h, wo)
            load("wi", wi_h, wit)
            load("wm", wm_h, wm)
            load("wg", wg_h, wgr.at[pl.ds(0, 3 * MUL)])
            load("wr", wr_h, wgr.at[pl.ds(3 * MUL, 3 * MUL)])
            load("wx", wx_h, wx)
            load("we", we_h, wer.at[:, pl.ds(0, C)])
            load("wrev", wrev_h, wer.at[:, pl.ds(C, C)])
            load("wc", wc_h, wc)
            loads["tensors"].wait()
        picked = dot(x[pl.ds(C, ROWS_T)], g[:, cols])
        own[pl.ds(C, ROWS_T), cols] = picked.astype(BF)
        for j in range(2):
            pack(picked[:, j * PAIR : (j + 1) * PAIR], 2 * half + j, send_b)
        for d in range(4 * half, 4 * half + 4):
            copies_b[d].start()

    loads["vectors"].wait()
    loads["species"].wait()
    v = [vec[k] for k in range(3)]
    high = [u.astype(BF).astype(F32) for u in v]
    middle = [(a - b).astype(BF).astype(F32) for a, b in zip(v, high)]
    low = [a - b - c for a, b, c in zip(v, high, middle)]
    species_row = spc[...].astype(F32)
    x[pl.ds(ROWS, EXTRA)] = jnp.concatenate(high + middle + low + [species_row] + [jnp.zeros_like(species_row)] * (EXTRA - 10), axis=0).astype(BF)
    extra = dot(x[pl.ds(ROWS, EXTRA)], g[...])
    own_vec = [extra[k : k + 1] + (extra[3 + k : 4 + k] + extra[6 + k : 7 + k]) for k in range(3)]
    own_species = extra[9:10]
    for pair in range(GROUPS):
        s = own_species[:, pair * PAIR : (pair + 1) * PAIR]
        send_s[2 * pair : 2 * pair + 1] = s
        send_s[2 * pair + 1 : 2 * pair + 2] = pltpu.roll(s, BLOCK, 1)
    for d in range(8):
        copies_s[d].start()

    loads["table"].wait()
    for j in range(4):
        for h in range(2):
            row = tab[j : j + 1, h * 128 : (h + 1) * 128]
            tb[j, pl.ds(h * 128, 128)] = jnp.broadcast_to(row, (128, 128)).T
    for name in ("reverse", "wq", "wk", "wv", "wo", "wi", "wm", "wg", "wr", "wx", "we", "wrev", "wc"):
        loads[name].wait()
    wi[...] = wit[...].astype(F32).T.astype(BF)

    weights = (wq, wkv, wo, wi, wm, wgr, wx, wer, wc)

    def columns(t):
        return pl.ds(t * TILE if isinstance(t, int) else pl.multiple_of(t * TILE, TILE), TILE)

    def gather(t, p, turned):
        p[...] = one_hot(E, 0, rev[:, columns(t)])
        turned[...] = dot(x[...], p[...]).astype(BF)

    def work(t, turned):
        cols = columns(t)
        here, there = x[pl.ds(0, C), cols], turned[pl.ds(0, C)]
        species_there = turned[pl.ds(ROWS, EXTRA)].astype(F32)[9:10]
        embedded = jnp.concatenate([embed(here, tb, spc[:, cols]), embed(there, tb, species_there)], axis=1)

        def store(k, new):
            out[pl.ds(C + k * MUL, MUL) if k >= 0 else pl.ds(0, C), cols] = new

        edge_update(
            lambda k: x[pl.ds(C + k * MUL, MUL), cols],
            lambda k: turned[pl.ds(C + k * MUL, MUL)],
            embedded,
            jnp.concatenate([there, here], axis=1),
            harmonics(vec[0, :, cols], vec[1, :, cols], vec[2, :, cols]),
            *weights,
            store,
        )

    def two_tiles(u, carry):
        gather(2 * u + 1, p1, rev1)
        work(2 * u, rev0)
        gather(2 * u + 2, p0, rev0)
        work(2 * u + 1, rev1)
        return carry

    tiles = E // TILE
    gather(0, p0, rev0)
    lax.fori_loop(0, tiles // 2 - 1, two_tiles, 0)
    gather(tiles - 1, p1, rev1)
    work(tiles - 2, rev0)
    work(tiles - 1, rev1)

    def unpack(a, b):
        a, b = a.astype(F32), b.astype(F32)
        top = jnp.where(lane < BLOCK, a, pltpu.roll(b, BLOCK, 1))
        bottom = jnp.where(lane < BLOCK, pltpu.roll(a, BLOCK, 1), b)
        return jnp.concatenate([top, bottom], axis=0).astype(BF)

    for pair in ARRIVAL:
        cols = pl.ds(pair * PAIR, PAIR)
        for d in (2 * pair, 2 * pair + 1):
            copies_a[OPPOSITE[d]].wait_recv()
            copies_s[OPPOSITE[d]].wait_recv()
        here = own[pl.ds(0, C), cols]
        there = unpack(recv_a[2 * pair], recv_a[2 * pair + 1])
        species_there = jnp.where(
            lane < BLOCK, recv_s[2 * pair : 2 * pair + 1], pltpu.roll(recv_s[2 * pair + 1 : 2 * pair + 2], BLOCK, 1)
        )
        species_both = jnp.concatenate([own_species[:, pair * PAIR : (pair + 1) * PAIR], species_there], axis=1)
        embedded = embed(jnp.concatenate([here, there], axis=1), tb, species_both)
        for d in (2 * pair, 2 * pair + 1):
            copies_b[OPPOSITE[d]].wait_recv()
        rev0[pl.ds(C, ROWS_T), pl.ds(0, PAIR)] = unpack(recv_b[2 * pair], recv_b[2 * pair + 1])

        def store(k, new):
            rows = pl.ds(C + k * MUL, MUL) if k >= 0 else pl.ds(0, C)
            if pair < 2:
                y[rows, cols] = new
            else:
                y_late[rows, pl.ds((pair - 2) * PAIR, PAIR)] = new

        edge_update(
            lambda k: own[pl.ds(C + k * MUL, MUL), cols],
            lambda k: rev0[pl.ds(C + k * MUL, MUL), pl.ds(0, PAIR)],
            embedded,
            jnp.concatenate([there, here], axis=1),
            harmonics(*[u[:, pair * PAIR : (pair + 1) * PAIR] for u in own_vec]),
            *weights,
            store,
        )
        if pair == 1:

            def place(t, carry):
                tile = columns(t)
                slot = slot_of(rev[:, tile])
                moved = dot(y[...], one_hot(EARLY, 0, slot)).astype(BF)
                out[:, tile] = jnp.where((slot >= 0) & (slot < EARLY), moved, out[:, tile])
                return carry

            lax.fori_loop(0, E // TILE, place, 0)
    for d in range(8):
        copies_a[d].wait_send()
        copies_b[d].wait_send()
        copies_s[d].wait_send()


CHUNKS = (192, 64, 192, 192, 192)


def final_kernel(part, last, reverse_h, scalars_h, tensors_h, done, rev, hot, load_sem, store_sem):
    load = pltpu.make_async_copy(reverse_h, rev, load_sem)
    load.start()
    load.wait()
    slot = slot_of(rev[...])
    hot[...] = one_hot(SLOTS - EARLY, EARLY, slot)
    stores = []
    start = 0
    for i, rows in enumerate(CHUNKS):
        for t in range(0, E, 512):
            moved = dot(last[pl.ds(start, rows)], hot[:, pl.ds(t, 512)]).astype(BF)
            block = (pl.ds(start, rows), pl.ds(t, 512))
            done[block] = jnp.where(slot[:, t : t + 512] >= EARLY, moved, part[block])
        dst = scalars_h.at[pl.ds(start, rows)] if start < C else tensors_h.at[pl.ds(start - C, rows)]
        copy = pltpu.make_async_copy(done.at[pl.ds(start, rows)], dst, store_sem.at[i])
        copy.start()
        stores.append(copy)
        start += rows
    for copy in stores:
        copy.wait()


def per_device(
    nx, ny,
    scalars, tensors, vectors, species, species_table, reverse, send_index, counts,
    w_query, w_key, w_value, w_output, w_invariant, w_message, w_gate, w_radial, w_mixing, w_expand, w_reverse, w_contract,
):
    reverse_row = reverse.reshape(1, E)
    hbm = pl.BlockSpec(memory_space=pltpu.HBM)
    vmem = pl.BlockSpec(memory_space=pltpu.VMEM)
    part, last = pl.pallas_call(
        functools.partial(exchange_kernel, nx, ny),
        out_shape=(pltpu.VMEM((ROWS, E), BF), pltpu.VMEM((ROWS, SLOTS - EARLY), BF)),
        in_specs=[hbm] * 19,
        out_specs=(vmem, vmem),
        scratch_shapes=[
            pltpu.VMEM((ROWS + EXTRA, E), BF),
            pltpu.VMEM((3, 1, E), F32),
            pltpu.VMEM((1, E), jnp.int32),
            pltpu.VMEM((4, C), F32),
            pltpu.VMEM((1, E), jnp.int32),
            pltpu.VMEM((8, BLOCK), jnp.int32),
            pltpu.VMEM((C, C), BF),
            pltpu.VMEM((2 * C, C), BF),
            pltpu.VMEM((C, C), BF),
            pltpu.VMEM((3 * MUL, C), BF),
            pltpu.VMEM((C, 3 * MUL), BF),
            pltpu.VMEM((C, C), BF),
            pltpu.VMEM((6 * MUL, C), BF),
            pltpu.VMEM((MUL, MUL), BF),
            pltpu.VMEM((FFN, 2 * C), BF),
            pltpu.VMEM((C, FFN), BF),
            pltpu.VMEM((E, SLOTS), BF),
            pltpu.VMEM((E, TILE), BF),
            pltpu.VMEM((E, TILE), BF),
            pltpu.VMEM((ROWS + EXTRA, TILE), BF),
            pltpu.VMEM((ROWS + EXTRA, TILE), BF),
            pltpu.VMEM((ROWS, SLOTS), BF),
            pltpu.VMEM((8, C // 2, 128), BF),
            pltpu.VMEM((8, ROWS_T // 2, 128), BF),
            pltpu.VMEM((8, C // 2, 128), BF),
            pltpu.VMEM((8, ROWS_T // 2, 128), BF),
            pltpu.VMEM((8, 128), F32),
            pltpu.VMEM((8, 128), F32),
            pltpu.VMEM((ROWS, EARLY), BF),
            pltpu.VMEM((4, C, 128), F32),
            pltpu.SemaphoreType.DMA((19,)),
            pltpu.SemaphoreType.DMA((3, 8)),
            pltpu.SemaphoreType.DMA((3, 8)),
        ],
        compiler_params=pltpu.CompilerParams(collective_id=0, has_side_effects=True, vmem_limit_bytes=int(60 * 2**20)),
        cost_estimate=pl.CostEstimate(flops=16 * 10**9, bytes_accessed=9 * 2**20, transcendentals=3 * 10**6),
        name="exchange",
    )(
        scalars.reshape(C, E), tensors.reshape(ROWS_T, E), vectors.reshape(3, 1, E), species.reshape(1, E),
        species_table.T, reverse_row, send_index.reshape(8, BLOCK),
        w_query, w_key, w_value, w_output, w_invariant.T, w_message, w_gate, w_radial, w_mixing,
        w_expand, w_reverse, w_contract,
    )
    new_scalars, new_tensors = pl.pallas_call(
        final_kernel,
        out_shape=(jax.ShapeDtypeStruct((C, E), BF), jax.ShapeDtypeStruct((ROWS_T, E), BF)),
        in_specs=[vmem, vmem, hbm],
        out_specs=(hbm, hbm),
        scratch_shapes=[
            pltpu.VMEM((ROWS, E), BF),
            pltpu.VMEM((1, E), jnp.int32),
            pltpu.VMEM((SLOTS - EARLY, E), BF),
            pltpu.SemaphoreType.DMA,
            pltpu.SemaphoreType.DMA((len(CHUNKS),)),
        ],
        compiler_params=pltpu.CompilerParams(vmem_limit_bytes=24 * 2**20),
        cost_estimate=pl.CostEstimate(flops=10**9, bytes_accessed=7 * 2**20, transcendentals=0),
        name="combine",
    )(part, last, reverse_row)
    return new_scalars.reshape(1, 1, C, E), new_tensors.reshape(1, 1, 9, MUL, E)


def solution(mesh):
    split = P("gx", "gy")
    return jax.shard_map(
        functools.partial(per_device, mesh.shape["gx"], mesh.shape["gy"]),
        mesh=mesh,
        in_specs=(split,) * 4 + (P(),) + (split,) * 3 + (P(),) * 12,
        out_specs=(split, split),
        check_vma=False,
    )
```

time: 58.8 us -> 50.6 us (0.86)
  the two profiles are of different devices: /device:TPU:1 before, /device:TPU:33 now
where the time goes in v1:
time: 50.6 us; the launch traced here: 50.5 us
  Pallas kernels  49.7 us (98%)
  between operations  0.82 us (2%)
    pallas_call x1, Pallas kernels, per_device(): pl.pallas_call(functools.partial(exchange_kernel, nx, ny), out_shape=(plt...  47.4 us
    pallas_call x1, Pallas kernels, per_device(): pl.pallas_call(final_kernel, out_shape=(jax.ShapeDtypeStruct((C, E), BF),...  2.31 us

profile of v1, /device:TPU:33, one launch (start us, length us, event | category | flops | bytes accessed | tf_op | source)
XLA Modules:
  0.0 50.5 jit_solution(16939235715986628797)
XLA Ops:
  0.6 0.0 copy-start
  0.6 47.4 %exchange.1 = (bf16[832,2048]{1,0:T(8,128)(2,1)S(1)}, bf16[832,256]{1,0:T(8,128)(2,1)S(1)}) custom-call(bf16[256,2048]{1,0:T(8,128)(2,1)} %bitcast.14, bf16[576,2048]{1,0:T(8,128)(2,1)} %bitcast.12, f32[3,1,2048]{2,1,0:T(1,128)} %bitcast.17, s32[1,2048]{1,0:T(1,128)} %bitcast.18, f32[4,256]{1,0:T(4,128)} %bitcast.19, s32[1,2048]{1,0:T(1,128)} %bitcast.10, ...), custom_call_target="tpu_custom_call" | custom-call | flops 16000000000 | bytes 9437184 | tf_op jit(solution)/shard_map/exchange/pallas_call | solution.py:363
  48.1 0.0 copy-done
  48.1 2.3 %combine.1 = (bf16[256,2048]{1,0:T(8,128)(2,1)}, bf16[576,2048]{1,0:T(8,128)(2,1)}) custom-call(bf16[832,2048]{1,0:T(8,128)(2,1)S(1)} %get-tuple-element.6.part, bf16[832,256]{1,0:T(8,128)(2,1)S(1)} %get-tuple-element.7.last, s32[1,2048]{1,0:T(1,128)S(1)} %bitcast.11), custom_call_target="tpu_custom_call" | custom-call | flops 1000000000 | bytes 7340032 | tf_op jit(solution)/shard_map/combine/pallas_call | solution.py:412
Async XLA Ops:
  0.6 47.4 %copy-start = (s32[1,1,2048]{2,1,0:T(1,128)S(1)}, s32[1,1,2048]{2,1,0:T(1,128)}, u32[]{:S(2)}) copy-start(s32[1,1,2048]{2,1,0:T(1,128)} %param.25) | copy-start | bytes 24580

commit v2 on v1

--- a/solution.py
+++ b/solution.py
@@ -25,7 +25,7 @@
 PAIR = 2 * BLOCK
 GROUPS = SLOTS // PAIR
 ARRIVAL = (0, 1, 3, 2)
-EARLY = 2 * PAIR
+EARLY = 0
 DEGREE = (0, 1, 1, 1, 2, 2, 2, 2, 2)
 BF = jnp.bfloat16
 F32 = jnp.float32
@@ -111,7 +111,7 @@
     x, vec, spc, tab, rev, sidx,
     wq, wkv, wo, wit, wi, wm, wgr, wx, wer, wc,
     g, p0, p1, rev0, rev1, own, send_a, send_b, recv_a, recv_b, send_s, recv_s,
-    y, tb,
+    tb,
     load_sem, send_sem, recv_sem,
 ):
     gx, gy = lax.axis_index("gx"), lax.axis_index("gy")
@@ -297,10 +297,7 @@
 
         def store(k, new):
             rows = pl.ds(C + k * MUL, MUL) if k >= 0 else pl.ds(0, C)
-            if pair < 2:
-                y[rows, cols] = new
-            else:
-                y_late[rows, pl.ds((pair - 2) * PAIR, PAIR)] = new
+            y_late[rows, cols] = new
 
         edge_update(
             lambda k: own[pl.ds(C + k * MUL, MUL), cols],
@@ -311,23 +308,13 @@
             *weights,
             store,
         )
-        if pair == 1:
-
-            def place(t, carry):
-                tile = columns(t)
-                slot = slot_of(rev[:, tile])
-                moved = dot(y[...], one_hot(EARLY, 0, slot)).astype(BF)
-                out[:, tile] = jnp.where((slot >= 0) & (slot < EARLY), moved, out[:, tile])
-                return carry
-
-            lax.fori_loop(0, E // TILE, place, 0)
     for d in range(8):
         copies_a[d].wait_send()
         copies_b[d].wait_send()
         copies_s[d].wait_send()
 
 
-CHUNKS = (192, 64, 192, 192, 192)
+CHUNKS = (128, 128, 192, 192, 128, 64)
 
 
 def final_kernel(part, last, reverse_h, scalars_h, tensors_h, done, rev, hot, load_sem, store_sem):
@@ -394,13 +381,12 @@
             pltpu.VMEM((8, ROWS_T // 2, 128), BF),
             pltpu.VMEM((8, 128), F32),
             pltpu.VMEM((8, 128), F32),
-            pltpu.VMEM((ROWS, EARLY), BF),
             pltpu.VMEM((4, C, 128), F32),
             pltpu.SemaphoreType.DMA((19,)),
             pltpu.SemaphoreType.DMA((3, 8)),
             pltpu.SemaphoreType.DMA((3, 8)),
         ],
-        compiler_params=pltpu.CompilerParams(collective_id=0, has_side_effects=True, vmem_limit_bytes=int(60 * 2**20)),
+        compiler_params=pltpu.CompilerParams(collective_id=0, has_side_effects=True, vmem_limit_bytes=59 * 2**20),
         cost_estimate=pl.CostEstimate(flops=16 * 10**9, bytes_accessed=9 * 2**20, transcendentals=3 * 10**6),
         name="exchange",
     )(

time: 50.6 us -> 49.3 us (0.974)
  Pallas kernels: 49.7 us -> 48.3 us
    pallas_call x1, Pallas kernels: 47.4 us -> 45.2 us  [per_device(): pl.pallas_call(functools.partial(exchange_kernel, nx, ny), out_shape=(plt...]
    pallas_call x1, Pallas kernels: 2.31 us -> 3.12 us  [per_device(): pl.pallas_call(final_kernel, out_shape=(jax.ShapeDtypeStruct((C, E), BF),...]
where the time goes in v2:
time: 49.3 us; the launch traced here: 49.2 us
  Pallas kernels  48.3 us (98%)
  between operations  0.82 us (2%)
    pallas_call x1, Pallas kernels, per_device(): pl.pallas_call(functools.partial(exchange_kernel, nx, ny), out_shape=(plt...  45.2 us
    pallas_call x1, Pallas kernels, per_device(): pl.pallas_call(final_kernel, out_shape=(jax.ShapeDtypeStruct((C, E), BF),...  3.12 us

profile of v2, /device:TPU:33, one launch (start us, length us, event | category | flops | bytes accessed | tf_op | source)
XLA Modules:
  0.0 49.2 jit_solution(10640144523469710870)
XLA Ops:
  0.6 0.0 copy-start
  0.6 45.2 %exchange.1 = (bf16[832,2048]{1,0:T(8,128)(2,1)S(1)}, bf16[832,512]{1,0:T(8,128)(2,1)S(1)}) custom-call(bf16[256,2048]{1,0:T(8,128)(2,1)} %bitcast.14, bf16[576,2048]{1,0:T(8,128)(2,1)} %bitcast.12, f32[3,1,2048]{2,1,0:T(1,128)} %bitcast.17, s32[1,2048]{1,0:T(1,128)} %bitcast.18, f32[4,256]{1,0:T(4,128)} %bitcast.19, s32[1,2048]{1,0:T(1,128)} %bitcast.10, ...), custom_call_target="tpu_custom_call" | custom-call | flops 16000000000 | bytes 9437184 | tf_op jit(solution)/shard_map/exchange/pallas_call | solution.py:350
  45.9 0.0 copy-done
  45.9 3.1 %combine.1 = (bf16[256,2048]{1,0:T(8,128)(2,1)}, bf16[576,2048]{1,0:T(8,128)(2,1)}) custom-call(bf16[832,2048]{1,0:T(8,128)(2,1)S(1)} %get-tuple-element.6.part, bf16[832,512]{1,0:T(8,128)(2,1)S(1)} %get-tuple-element.7.last, s32[1,2048]{1,0:T(1,128)S(1)} %bitcast.11), custom_call_target="tpu_custom_call" | custom-call | flops 1000000000 | bytes 7340032 | tf_op jit(solution)/shard_map/combine/pallas_call | solution.py:398
Async XLA Ops:
  0.6 45.2 %copy-start = (s32[1,1,2048]{2,1,0:T(1,128)S(1)}, s32[1,1,2048]{2,1,0:T(1,128)}, u32[]{:S(2)}) copy-start(s32[1,1,2048]{2,1,0:T(1,128)} %param.25) | copy-start | bytes 24580
